TPU v7x, 768 devices: a whole 4x8x12 slice. The times are simulated.
768 devices in a mesh: outer: 96 (over x, y, z_hi), inner: 8 (over z_lo, core).
Axes of the slice: x: 4, y: 8, z: 12 (z_hi: 3, z_lo: 4; z = z_hi * 4 + z_lo), core: 2. Of those that a mesh axis runs over, the one named last changes fastest.
Arguments:
- x_normed: bfloat16 [393216, 3840], P(('outer', 'inner')), may hold values from -24 to 24
- key_grad: bfloat16 [393216, 128], P(('outer', 'inner')), may hold values from -0.009765625 to 0.009765625
- value_grad: bfloat16 [393216, 128], P(('outer', 'inner')), may hold values from -0.009765625 to 0.009765625
Outputs:
- key_weight_grad: float32 [3840, 128], P(('outer', 'inner'))
- value_weight_grad: float32 [3840, 128], P(('outer', 'inner'))
All inputs are finite; a program needn't handle non-finite values.
Results may differ from a plain program's by a relative error of at most 0.0029.
Values may be sent and summed in bfloat16 or wider, within the bound.
A program may use at most 32 MiB of HBM per device.

v0:
```python
import jax
import jax.numpy as jnp
from jax import lax
from jax.sharding import PartitionSpec as P


def local_partial(inputs, cotangent):
    product = lax.dot_general(
        inputs, cotangent, (((0,), (0,)), ((), ())), preferred_element_type=jnp.float32
    )
    return product.astype(jnp.bfloat16)


def per_device(x_normed, key_grad, value_grad):
    key_part = local_partial(x_normed, key_grad)
    value_part = local_partial(x_normed, value_grad)
    key_wide = lax.optimization_barrier(key_part).astype(jnp.float32)
    value_wide = lax.optimization_barrier(value_part).astype(jnp.float32)
    key_total, value_total = (
        lax.psum_scatter(key_wide, ("outer", "inner"), scatter_dimension=0, tiled=True),
        lax.psum_scatter(value_wide, ("outer", "inner"), scatter_dimension=0, tiled=True),
    )
    return (key_total, value_total)


def solution(mesh):
    return jax.shard_map(
        per_device,
        mesh=mesh,
        in_specs=(
            P(("outer", "inner"), None),
            P(("outer", "inner"), None),
            P(("outer", "inner"), None),
        ),
        out_specs=(P(("outer", "inner"), None), P(("outer", "inner"), None)),
        check_vma=False,
    )
```

profile of v0, /device:TPU:1, one launch (start us, length us, event | category | flops | bytes accessed | tf_op | source)
XLA Modules:
  0.0 147.3 jit_solution(2782576466940471877)
XLA Ops:
  0.6 0.0 copy-start
  0.6 0.0 copy-start.1
  0.7 0.9 copy-done
  1.5 0.0 copy-start.2
  1.5 3.7 %convolution_convert_fusion.1 = bf16[3840,128]{1,0:T(8,128)(2,1)S(1)} fusion(bf16[512,3840]{1,0:T(8,128)(2,1)} %param.3, bf16[512,128]{1,0:T(8,128)(2,1)S(1)} %copy-done), kind=kOutput, calls=%fused_computation.1 | convolution fusion | flops 503808000 | bytes 5046272 | tf_op jit(solution)/shard_map/dot_general | solution.py:8
  5.2 0.0 copy-done.1
  5.2 0.0 copy-done.2
  5.3 1.2 convolution_convert_fusion
  6.5 139.4 %all-reduce.4 = (f32[3840,128]{1,0:T(8,128)}, f32[3840,128]{1,0:T(8,128)}) all-reduce(bf16[3840,128]{1,0:T(8,128)(2,1)S(1)} %convolution_convert_fusion.1, bf16[3840,128]{1,0:T(8,128)(2,1)S(1)} %convolution_convert_fusion), channel_id=2, replica_groups=mesh['outer'=96,'inner'=8] {'outer','inner'}, use_global_device_ids=true, to_apply=%region_0.0.clone | all-reduce | flops 983040 | bytes 5898240
  145.9 1.3 constant_dynamic-slice_fusion
Async XLA Ops:
  0.6 0.9 copy-start
  0.6 4.6 %copy-start.1 = (bf16[512,3840]{1,0:T(8,128)(2,1)S(1)}, bf16[512,3840]{1,0:T(8,128)(2,1)}, u32[]{:S(2)}) copy-start(bf16[512,3840]{1,0:T(8,128)(2,1)} %param.3) | copy-start | bytes 11796484
  1.5 3.7 %copy-start.2 = (bf16[512,128]{1,0:T(8,128)(2,1)S(1)}, bf16[512,128]{1,0:T(8,128)(2,1)}, u32[]{:S(2)}) copy-start(bf16[512,128]{1,0:T(8,128)(2,1)} %param.5) | copy-start | bytes 393220
where the time goes:
time: 148 us; the launch traced here: 147 us
  blocking collectives  139 us (94%)
  matrix products  4.93 us (3%)
  local copies, waits for them, and re-layouts  2.22 us (2%)
    unnamed x1, blocking collectives  139 us
    dot_general x2, matrix products, local_partial(): lax.dot_general(inputs, cotangent, (((0,), (0,)), ((), ())), preferred_el...  4.93 us

commit v1 on v0

v1 whole, which is shorter than its diff:
```python
import jax
import jax.numpy as jnp
from jax import lax
from jax.experimental import pallas as pl
from jax.experimental.pallas import tpu as pltpu
from jax.sharding import PartitionSpec as P

MESH = pl.DeviceIdType.MESH
NX, NY, NZ = 4, 8, 12
D_WIN, HEAD, TOK = 3840, 128, 512
PAIR = 240
ROWS = 120
PAD = 128
OWN = 5
LOAD = 768
COLS = 256
bf16, f32 = jnp.bfloat16, jnp.float32


def device(x, y, z, core):
    return ((x * NY + y) * 3 + z // 4, (z % 4) * 2 + core)


def kernel(
    x_hbm, k_hbm, v_hbm, out, xv, g, give, keep, got, xs, xr, ysum, ys, yr, total, zs, zr,
    load_sem, core_send, core_recv, x_send, x_recv, y_send, y_recv, z_send, z_recv,
):
    outer, inner = lax.axis_index("outer"), lax.axis_index("inner")
    x, y = outer // (NY * 3), (outer // 3) % NY
    z, core = (outer % 3) * 4 + inner // 2, inner % 2
    other = 1 - core

    loads = [pltpu.make_async_copy(k_hbm, g.at[0], load_sem.at[0]), pltpu.make_async_copy(v_hbm, g.at[1], load_sem.at[1])]
    for n in range(D_WIN // LOAD):
        part = pl.ds(n * LOAD, LOAD)
        loads.append(pltpu.make_async_copy(x_hbm.at[:, part], xv.at[:, part], load_sem.at[2 + n]))
    for copy in loads:
        copy.start()

    peers = [device(x, y, z, other)]
    peers += [device((x + d) % NX, y, z, core) for d in range(1, NX)]
    peers += [device(x, (y + d) % NY, z, core) for d in range(1, NY)]
    peers += [device(x, y, (z + d) % NZ, c) for d in range(1, NZ) for c in range(2)]
    barrier = pltpu.get_barrier_semaphore()
    for peer in peers:
        pl.semaphore_signal(barrier, inc=1, device_id=peer, device_id_type=MESH)

    loads[0].wait()
    loads[1].wait()
    gt = jnp.concatenate([g[other].T, g[core].T], axis=0)
    for n in range(D_WIN // COLS):
        if n % (LOAD // COLS) == 0:
            loads[2 + n // (LOAD // COLS)].wait()
        part = jnp.dot(gt, xv[:, n * COLS : (n + 1) * COLS], preferred_element_type=f32).astype(bf16)
        for half, dest in ((part[:HEAD].T, give), (part[HEAD:].T, keep)):
            at = n * COLS
            while at < (n + 1) * COLS:
                end = min((at // PAIR + 1) * PAIR, (n + 1) * COLS)
                pair, lo = at // PAIR, at % PAIR
                dest[pair // 4, pair % 4, lo : lo + end - at, :] = half[at - n * COLS : end - n * COLS]
                at = end
    pl.semaphore_wait(barrier, len(peers))

    def remote(src, dst, send, recv, to):
        return pltpu.make_async_remote_copy(
            src_ref=src, dst_ref=dst, send_sem=send, recv_sem=recv, device_id=to, device_id_type=MESH
        )

    mine = y // 2
    order = [(mine + d) % 4 for d in (2, 1, 3, 0)]
    swaps = []
    for p, q in enumerate(order):
        swaps.append(remote(give.at[:, q], got.at[p], core_send.at[p], core_recv.at[p], peers[0]))
        swaps[p].start()

    sent = []

    def along_x(p):
        swaps[p].wait_recv()
        q = order[p]
        for n in range(NX):
            xs[p, n] = (keep[n, q].astype(f32) + got[p, n].astype(f32)).astype(bf16)
        for d in (2, 1, 3):
            to = (x + d) % NX
            copy = remote(xs.at[p, to], xr.at[p, d - 1], x_send.at[p, d - 1], x_recv.at[p], device(to, y, z, core))
            copy.start()
            sent.append(copy)

    def along_y(p):
        pltpu.make_async_copy(xr.at[p], xr.at[p], x_recv.at[p]).wait()
        s = xs[p, x].astype(f32)
        for d in range(NX - 1):
            s += xr[p, d].astype(f32)
        if p < 3:
            for j in range(2):
                ys[p, j, :ROWS] = s[j * ROWS : (j + 1) * ROWS].astype(bf16)
            for j in range(2):
                to = order[p] * 2 + j
                copy = remote(
                    ys.at[p, j], yr.at[(y - to + NY) % NY - 1], y_send.at[p, j], y_recv, device(x, to, z, core)
                )
                copy.start()
                sent.append(copy)
        else:
            for j in range(2):
                ysum[j] = s[j * ROWS : (j + 1) * ROWS]
            own, j = y % 2, 1 - y % 2
            ys[p, 0, :ROWS] = ysum[j].astype(bf16)
            to = order[p] * 2 + j
            copy = remote(
                ys.at[p, 0], yr.at[(y - to + NY) % NY - 1], y_send.at[p, 0], y_recv, device(x, to, z, core)
            )
            copy.start()
            sent.append(copy)

    for p in range(4):
        along_x(p)
        if p >= 1:
            along_y(p - 1)
    along_y(3)

    pltpu.make_async_copy(yr, yr, y_recv).wait()
    s = ysum[y % 2]
    for d in range(NY - 1):
        s += yr[d, :ROWS].astype(f32)
    total[...] = s
    for n in range(2 * NZ):
        zs[n, :OWN] = total[n * OWN : (n + 1) * OWN]
    for d in (6, 5, 7, 4, 8, 3, 9, 2, 10, 1, 11, 0):
        to = (z + d) % NZ
        for c in (0, 1) if d else (0,):
            c = c if d else other
            copy = remote(
                zs.at[to * 2 + c, pl.ds(0, OWN)],
                zr.at[core * NZ + d, pl.ds(0, OWN)],
                z_send.at[d * 2 + (c if d else 0)],
                z_recv,
                device(x, y, to, c),
            )
            copy.start()
            sent.append(copy)
    zr[core * NZ, :OWN] = zs[z * 2 + core, :OWN]
    got_all = zr.at[pl.ds(0, 2 * NZ - 1), pl.ds(0, OWN)]
    pltpu.make_async_copy(got_all, got_all, z_recv).wait()
    for t in range(2):
        s = zr[t * NZ, :OWN]
        for d in range(1, NZ):
            s += zr[t * NZ + d, :OWN]
        out[t, :OWN] = s
    for copy in swaps + sent:
        copy.wait_send()


def split(both, key_out, value_out):
    key_out[...] = both[0, :OWN]
    value_out[...] = both[1, :OWN]


def per_device(x_normed, key_grad, value_grad):
    hbm = pl.BlockSpec(memory_space=pl.ANY)
    vmem = pl.BlockSpec(memory_space=pltpu.VMEM)
    dma = pltpu.SemaphoreType.DMA
    both = pl.pallas_call(
        kernel,
        out_shape=jax.ShapeDtypeStruct((2, 8, HEAD), f32),
        in_specs=[hbm] * 3,
        out_specs=vmem,
        scratch_shapes=[
            pltpu.VMEM((TOK, D_WIN), bf16),
            pltpu.VMEM((2, TOK, HEAD), bf16),
            pltpu.VMEM((NX, 4, PAIR, HEAD), bf16),
            pltpu.VMEM((NX, 4, PAIR, HEAD), bf16),
            pltpu.VMEM((4, NX, PAIR, HEAD), bf16),
            pltpu.VMEM((4, NX, PAIR, HEAD), bf16),
            pltpu.VMEM((4, NX - 1, PAIR, HEAD), bf16),
            pltpu.VMEM((2, ROWS, HEAD), f32),
            pltpu.VMEM((4, 2, PAD, HEAD), bf16),
            pltpu.VMEM((NY - 1, PAD, HEAD), bf16),
            pltpu.VMEM((ROWS, HEAD), f32),
            pltpu.VMEM((2 * NZ, 8, HEAD), f32),
            pltpu.VMEM((2 * NZ, 8, HEAD), f32),
            dma((2 + D_WIN // LOAD,)),
            dma((4,)),
            dma((4,)),
            dma((4, NX - 1)),
            dma((4,)),
            dma((4, 2)),
            dma,
            dma((2 * NZ,)),
            dma,
        ],
        compiler_params=pltpu.CompilerParams(
            collective_id=0, has_side_effects=True, vmem_limit_bytes=60 * 1024 * 1024
        ),
    )(x_normed, key_grad, value_grad)
    owned = jax.ShapeDtypeStruct((OWN, HEAD), f32)
    return pl.pallas_call(split, out_shape=(owned, owned), in_specs=[vmem], out_specs=(vmem, vmem))(both)


def solution(mesh):
    rows = P(("outer", "inner"), None)
    return jax.shard_map(per_device, mesh=mesh, in_specs=(rows,) * 3, out_specs=(rows, rows), check_vma=False)
```

time: 148 us -> 46 us (0.31)
  blocking collectives: 139 us -> 0 us
  Pallas kernels: 0 us -> 44.9 us
  matrix products: 4.93 us -> 0 us
  local copies, waits for them, and re-layouts: 2.22 us -> 0 us
    unnamed x1 -> x0, blocking collectives: 139 us -> none
    pallas_call x0 -> x2, Pallas kernels: none -> 44.9 us  [the longest x1 43.7 us: per_device(): pl.pallas_call(kernel, out_shape=jax.ShapeDtypeStruct((2, 8, HEAD), f32),...]
    dot_general x2 -> x0, matrix products: 4.93 us -> none  [local_partial(): lax.dot_general(inputs, cotangent, (((0,), (0,)), ((), ())), preferred_el...]
    unnamed x7 -> x0, local copies, waits for them, and re-layouts: 2.22 us -> none
where the time goes in v1:
time: 46 us; the launch traced here: 45.6 us
  Pallas kernels  44.9 us (98%)
  between operations  0.64 us (1%)
    pallas_call x1, Pallas kernels, per_device(): pl.pallas_call(kernel, out_shape=jax.ShapeDtypeStruct((2, 8, HEAD), f32),...  43.7 us
    pallas_call x1, Pallas kernels, per_device(): pl.pallas_call(split, out_shape=(owned, owned), in_specs=[vmem], out_spec...  1.3 us

profile of v1, /device:TPU:1, one launch (start us, length us, event | category | flops | bytes accessed | tf_op | source)
XLA Modules:
  0.0 45.6 jit_solution(12636394968444585788)
XLA Ops:
  0.6 43.7 %shard_map.50.both = f32[2,8,128]{2,1,0:T(8,128)} custom-call(bf16[512,3840]{1,0:T(8,128)(2,1)} %x_hbm.1, bf16[512,128]{1,0:T(8,128)(2,1)} %k_hbm.1, bf16[512,128]{1,0:T(8,128)(2,1)} %v_hbm.1), custom_call_target="tpu_custom_call" | custom-call | tf_op jit(solution)/shard_map/pallas_call | solution.py:163
  44.3 1.3 %shard_map.51 = (f32[5,128]{1,0:T(8,128)}, f32[5,128]{1,0:T(8,128)}) custom-call(f32[2,8,128]{2,1,0:T(8,128)} %shard_map.50.both), custom_call_target="tpu_custom_call" | custom-call | tf_op jit(solution)/shard_map/pallas_call | solution.py:197

commit v2 on v0

v2 whole, which is shorter than its diff:
```python
import jax
import jax.numpy as jnp
from jax import lax
from jax.experimental import pallas as pl
from jax.experimental.pallas import tpu as pltpu
from jax.sharding import PartitionSpec as P

MESH = pl.DeviceIdType.MESH
NX, NY, NZ = 4, 8, 12
D_WIN, HEAD, TOK = 3840, 128, 512
ROWS = 120
OWN = 5
LOAD = 768
COLS = 256
PIECES = ((0, 16), (16, 32), (32, 64), (64, 96), (96, 120))
HEIGHTS = tuple(-(-(hi - lo) // 16) * 16 for lo, hi in PIECES)
ORDER = ("x0", "x1", "x2", "x3", "x4", "y0", "y1", "y2", "z0", "z1", "y3", "z2", "y4", "z3", "z4")
bf16, f32 = jnp.bfloat16, jnp.float32


def device(x, y, z, core):
    return ((x * NY + y) * 3 + z // 4, (z % 4) * 2 + core)


def kernel(x_hbm, k_hbm, v_hbm, out, xv, g, give, keep, got, xs, xr, yf, ys, yr, total, zs, zr, load_sem, core_send,
           core_recv, x_send, x_recv, y_send, y_recv, z_send, z_recv, plane_in, line_in):
    outer, inner = lax.axis_index("outer"), lax.axis_index("inner")
    x, y = outer // (NY * 3), (outer // 3) % NY
    z, core = (outer % 3) * 4 + inner // 2, inner % 2
    other = 1 - core

    loads = [pltpu.make_async_copy(k_hbm, g.at[0], load_sem.at[0]), pltpu.make_async_copy(v_hbm, g.at[1], load_sem.at[1])]
    for n in range(D_WIN // LOAD):
        part = pl.ds(n * LOAD, LOAD)
        loads.append(pltpu.make_async_copy(x_hbm.at[:, part], xv.at[:, part], load_sem.at[2 + n]))
    for copy in loads:
        copy.start()

    barrier = pltpu.get_barrier_semaphore()

    def signal(sem, to):
        pl.semaphore_signal(sem, inc=1, device_id=to, device_id_type=MESH)

    for d in (4, 3, 5, 2, 6, 1, 7):
        signal(barrier, device(x, (y + d) % NY, z, 0))
    for d in (2, 1, 3):
        signal(barrier, device((x + d) % NX, y, z, 0))

    @pl.when(core == 1)
    def _():
        signal(barrier, device(x, y, z, 0))

    for d in (6, 5, 7, 4, 8, 3, 9, 2, 10, 1, 11):
        signal(barrier, device(x, y, (z + d) % NZ, 1))

    loads[0].wait()
    loads[1].wait()
    gt = jnp.concatenate([g[other].T, g[core].T], axis=0)
    for n in range(D_WIN // COLS):
        if n % (LOAD // COLS) == 0:
            loads[2 + n // (LOAD // COLS)].wait()
        start, stop = n * COLS, (n + 1) * COLS
        part = jnp.dot(gt, xv[:, start:stop], preferred_element_type=f32).astype(bf16)
        for half, dest in ((part[:HEAD].T, give), (part[HEAD:].T, keep)):
            for block in range(start // ROWS, -(-stop // ROWS)):
                for p, (lo, hi) in enumerate(PIECES):
                    first, last = max(start, block * ROWS + lo), min(stop, block * ROWS + hi)
                    if first < last:
                        at = first - block * ROWS - lo
                        dest[p][block // NY, block % NY, at : at + last - first, :] = half[first - start : last - start]

    @pl.when(core == 0)
    def _():
        pl.semaphore_wait(barrier, 2 * (NX - 1) + 2 * (NY - 1) + 1)
        signal(plane_in, device(x, y, z, 1))

    @pl.when(core == 1)
    def _():
        pl.semaphore_wait(plane_in, 1)

    def remote(src, dst, send, recv, to):
        return pltpu.make_async_remote_copy(
            src_ref=src, dst_ref=dst, send_sem=send, recv_sem=recv, device_id=to, device_id_type=MESH
        )

    def wait(ref, sem):
        pltpu.make_async_copy(ref, ref, sem).wait()

    swaps = [
        remote(give[p], got[p], core_send.at[p], core_recv.at[p], device(x, y, z, other)) for p in range(len(PIECES))
    ]
    for swap in swaps:
        swap.start()

    def along_x(p):
        swaps[p].wait_recv()
        for n in range(NX):
            xs[p][n] = (keep[p][n].astype(f32) + got[p][n].astype(f32)).astype(bf16)
        for d in (2, 1, 3):
            to = (x + d) % NX
            remote(xs[p].at[to], xr[p].at[d - 1], x_send.at[p], x_recv.at[p], device(to, y, z, core)).start()

    def along_y(p):
        wait(xr[p], x_recv.at[p])
        s = keep[p][x].astype(f32) + got[p][x].astype(f32)
        for d in range(NX - 1):
            s += xr[p][d].astype(f32)
        yf[p][...] = s
        ys[p][...] = s.astype(bf16)
        for d in (4, 3, 5, 2, 6, 1, 7):
            to = (y + d) % NY
            remote(ys[p].at[to], yr[p].at[d - 1], y_send.at[p], y_recv.at[p], device(x, to, z, core)).start()

    def along_z(p):
        wait(yr[p], y_recv.at[p])
        s = yf[p][y]
        for d in range(NY - 1):
            s += yr[p][d].astype(f32)
        lo, hi = PIECES[p]
        total[lo : lo + HEIGHTS[p]] = s
        for to in range(NZ):
            if not lo < (to + 1) * 2 * OWN <= hi:
                continue
            for c in range(2):
                n = to * 2 + c
                zs[n, :OWN] = total[n * OWN : (n + 1) * OWN]

                @pl.when(jnp.logical_or(z != to, core != c))
                def _():
                    src, dst = zs.at[n, pl.ds(0, OWN)], zr.at[core * NZ + z, pl.ds(0, OWN)]
                    remote(src, dst, z_send, z_recv, device(x, y, to, c)).start()

    def meet_z():
        @pl.when(core == 1)
        def _():
            pl.semaphore_wait(barrier, 2 * (NZ - 1))
            signal(line_in, device(x, y, z, 0))

        @pl.when(core == 0)
        def _():
            pl.semaphore_wait(line_in, 1)

    steps = {"x": along_x, "y": along_y, "z": along_z}
    for step in ORDER:
        if step == "z0":
            meet_z()
        steps[step[0]](int(step[1]))

    zr[core * NZ + z, :OWN] = zs[z * 2 + core, :OWN]
    for p in range(len(PIECES)):
        swaps[p].wait_send()
        wait(xr[p], x_send.at[p])
        wait(yr[p], y_send.at[p])
    all_but_one = zr.at[pl.ds(0, 2 * NZ - 1), pl.ds(0, OWN)]
    wait(all_but_one, z_send)
    wait(all_but_one, z_recv)
    for t in range(2):
        s = zr[t * NZ, :OWN]
        for d in range(1, NZ):
            s += zr[t * NZ + d, :OWN]
        out[t, :OWN] = s


def split(both, key_out, value_out):
    key_out[...] = both[0, :OWN]
    value_out[...] = both[1, :OWN]


def per_device(x_normed, key_grad, value_grad):
    hbm = pl.BlockSpec(memory_space=pl.ANY)
    vmem = pl.BlockSpec(memory_space=pltpu.VMEM)
    dma = pltpu.SemaphoreType.DMA
    count = len(PIECES)

    def buffers(*dims, dtype=bf16):
        return [pltpu.VMEM((*dims, height, HEAD), dtype) for height in HEIGHTS]

    both = pl.pallas_call(
        kernel,
        out_shape=jax.ShapeDtypeStruct((2, 8, HEAD), f32),
        in_specs=[hbm] * 3,
        out_specs=vmem,
        scratch_shapes=[
            pltpu.VMEM((TOK, D_WIN), bf16),
            pltpu.VMEM((2, TOK, HEAD), bf16),
            buffers(NX, NY),
            buffers(NX, NY),
            buffers(NX, NY),
            buffers(NX, NY),
            buffers(NX - 1, NY),
            buffers(NY, dtype=f32),
            buffers(NY),
            buffers(NY - 1),
            pltpu.VMEM((128, HEAD), f32),
            pltpu.VMEM((2 * NZ, 8, HEAD), f32),
            pltpu.VMEM((2 * NZ, 8, HEAD), f32),
            dma((2 + D_WIN // LOAD,)),
            dma((count,)),
            dma((count,)),
            dma((count,)),
            dma((count,)),
            dma((count,)),
            dma((count,)),
            dma,
            dma,
            pltpu.SemaphoreType.REGULAR,
            pltpu.SemaphoreType.REGULAR,
        ],
        compiler_params=pltpu.CompilerParams(
            collective_id=0, has_side_effects=True, vmem_limit_bytes=60 * 1024 * 1024
        ),
    )(x_normed, key_grad, value_grad)
    owned = jax.ShapeDtypeStruct((OWN, HEAD), f32)
    return pl.pallas_call(split, out_shape=(owned, owned), in_specs=[vmem], out_specs=(vmem, vmem))(both)


def solution(mesh):
    rows = P(("outer", "inner"), None)
    return jax.shard_map(per_device, mesh=mesh, in_specs=(rows,) * 3, out_specs=(rows, rows), check_vma=False)
```

time: 148 us -> 39.4 us (0.27)
  the two profiles are of different devices: /device:TPU:1 before, /device:TPU:193 now
where the time goes in v2:
time: 39.4 us; the launch traced here: 39.2 us
  Pallas kernels  38.6 us (98%)
  between operations  0.64 us (2%)
    pallas_call x1, Pallas kernels, per_device(): pl.pallas_call(kernel, out_shape=jax.ShapeDtypeStruct((2, 8, HEAD), f32),...  37.3 us
    pallas_call x1, Pallas kernels, per_device(): pl.pallas_call(split, out_shape=(owned, owned), in_specs=[vmem], out_spec...  1.3 us

profile of v2, /device:TPU:193, one launch (start us, length us, event | category | flops | bytes accessed | tf_op | source)
XLA Modules:
  0.0 39.2 jit_solution(11991647737675907859)
XLA Ops:
  0.6 37.3 %shard_map.50.both = f32[2,8,128]{2,1,0:T(8,128)} custom-call(bf16[512,3840]{1,0:T(8,128)(2,1)} %x_hbm.1, bf16[512,128]{1,0:T(8,128)(2,1)} %k_hbm.1, bf16[512,128]{1,0:T(8,128)(2,1)} %v_hbm.1), custom_call_target="tpu_custom_call" | custom-call | tf_op jit(solution)/shard_map/pallas_call | solution.py:178
  37.9 1.3 %shard_map.51 = (f32[5,128]{1,0:T(8,128)}, f32[5,128]{1,0:T(8,128)}) custom-call(f32[2,8,128]{2,1,0:T(8,128)} %shard_map.50.both), custom_call_target="tpu_custom_call" | custom-call | tf_op jit(solution)/shard_map/pallas_call | solution.py:214

commit v3 on v2

v3 whole, which is shorter than its diff:
```python
import jax
import jax.numpy as jnp
from jax import lax
from jax.experimental import pallas as pl
from jax.experimental.pallas import tpu as pltpu
from jax.sharding import PartitionSpec as P

MESH = pl.DeviceIdType.MESH
NX, NY, NZ = 4, 8, 12
D_WIN, HEAD, TOK = 3840, 128, 512
ROWS = 120
OWN = 5
LOADS = (2560, 1280)
COLS = 256
PIECES = (
    (0, 0, 16), (0, 16, 32), (1, 0, 16), (0, 32, 48), (1, 16, 32), (0, 48, 64), (1, 32, 64), (0, 64, 96), (1, 64, 80), (0, 96, 120), (1, 80, 120),
)
HEIGHTS = tuple(-(-(hi - lo) // 16) * 16 for _, lo, hi in PIECES)
GROUP = 4
ORDER = (
    "c0", "c1", "x0", "c2", "x1", "c3", "x2", "c4", "x3", "c5", "x4", "c6", "x5", "c7", "x6", "c8", "x7", "y0",
    "c9", "x8", "c10", "x9", "y1", "x10", "y2", "y3", "m0", "y4", "y5", "m1", "z0", "y6", "z1", "z2", "y7",
    "z3", "z4", "z5", "y8", "z6", "y9", "z7", "z8", "y10", "z9", "z10",
)
bf16, f32 = jnp.bfloat16, jnp.float32


def device(x, y, z, core):
    return ((x * NY + y) * 3 + z // 4, (z % 4) * 2 + core)


def kernel(x_hbm, k_hbm, v_hbm, out, xv, g, give, keep, got, xs, xr, yf, ys, yr, total, zs, zr, load_sem, core_send,
           core_recv, x_send, x_recv, y_send, y_recv, z_send, z_recv, plane_in, line_in):
    outer, inner = lax.axis_index("outer"), lax.axis_index("inner")
    x, y = outer // (NY * 3), (outer // 3) % NY
    z, core = (outer % 3) * 4 + inner // 2, inner % 2
    other = 1 - core

    loads = [pltpu.make_async_copy(k_hbm, g.at[0], load_sem.at[0]), pltpu.make_async_copy(v_hbm, g.at[1], load_sem.at[1])]
    segments, at = [], 0
    for n, width in enumerate(LOADS):
        segments.append((at, at + width))
        part = pl.ds(at, width)
        loads.append(pltpu.make_async_copy(x_hbm.at[:, part], xv.at[:, part], load_sem.at[2 + n]))
        at += width
    for copy in loads:
        copy.start()

    barrier = pltpu.get_barrier_semaphore()

    def signal(sem, to):
        pl.semaphore_signal(sem, inc=1, device_id=to, device_id_type=MESH)

    for d in (4, 3, 5, 2, 6, 1, 7):
        signal(barrier, device(x, (y + d) % NY, z, 0))
    for d in (2, 1, 3):
        signal(barrier, device((x + d) % NX, y, z, 0))

    @pl.when(core == 1)
    def _():
        signal(barrier, device(x, y, z, 0))

    for d in (6, 5, 7, 4, 8, 3, 9, 2, 10, 1, 11):
        signal(barrier, device(x, y, (z + d) % NZ, 1))

    def meet_plane():
        @pl.when(core == 0)
        def _():
            pl.semaphore_wait(barrier, 2 * (NX - 1) + 2 * (NY - 1) + 1)
            signal(plane_in, device(x, y, z, 1))

    loads[0].wait()
    loads[1].wait()
    gt = jnp.concatenate([g[other].T, g[core].T], axis=0)
    for n in range(D_WIN // COLS):
        start, stop = n * COLS, (n + 1) * COLS
        for m, (first, last) in enumerate(segments):
            if start == first:
                if m == len(segments) - 1:
                    meet_plane()
                loads[2 + m].wait()
        part = jnp.dot(gt, xv[:, start:stop], preferred_element_type=f32).astype(bf16)
        for half, dest in ((part[:HEAD].T, give), (part[HEAD:].T, keep)):
            for block in range(start // ROWS, -(-stop // ROWS)):
                for p, (group, lo, hi) in enumerate(PIECES):
                    first, last = max(start, block * ROWS + lo), min(stop, block * ROWS + hi)
                    if first < last and block % NY // GROUP == group:
                        at = first - block * ROWS - lo
                        dest[p][block // NY, block % GROUP, at : at + last - first, :] = half[first - start : last - start]


    @pl.when(core == 1)
    def _():
        pl.semaphore_wait(plane_in, 1)

    def remote(src, dst, send, recv, to):
        return pltpu.make_async_remote_copy(
            src_ref=src, dst_ref=dst, send_sem=send, recv_sem=recv, device_id=to, device_id_type=MESH
        )

    def wait(ref, sem):
        pltpu.make_async_copy(ref, ref, sem).wait()

    swaps = [
        remote(give[p], got[p], core_send.at[p], core_recv.at[p], device(x, y, z, other)) for p in range(len(PIECES))
    ]

    def swap_cores(p):
        swaps[p].start()

    def along_x(p):
        swaps[p].wait_recv()
        for n in range(NX):
            xs[p][n] = (keep[p][n].astype(f32) + got[p][n].astype(f32)).astype(bf16)
        for d in (2, 1, 3):
            to = (x + d) % NX
            remote(xs[p].at[to], xr[p].at[d - 1], x_send.at[p], x_recv.at[p], device(to, y, z, core)).start()

    def along_y(p):
        wait(xr[p], x_recv.at[p])
        s = keep[p][x].astype(f32) + got[p][x].astype(f32)
        for d in range(NX - 1):
            s += xr[p][d].astype(f32)
        yf[p][...] = s
        ys[p][...] = s.astype(bf16)
        for n in range(GROUP):
            to = PIECES[p][0] * GROUP + n

            @pl.when(y != to)
            def _():
                slot = (y - to + NY) % NY - 1
                remote(ys[p].at[n], yr[p].at[slot], y_send.at[p], y_recv.at[p], device(x, to, z, core)).start()

    def along_z(p):
        @pl.when(y // GROUP == PIECES[p][0])
        def _():
            wait(yr[p], y_recv.at[p])
            s = yf[p][y % GROUP]
            for d in range(NY - 1):
                s += yr[p][d].astype(f32)
            _, lo, hi = PIECES[p]
            total[lo : lo + HEIGHTS[p]] = s
            for to in range(NZ):
                if not lo < (to + 1) * 2 * OWN <= hi:
                    continue
                for c in range(2):
                    n = to * 2 + c
                    zs[n, :OWN] = total[n * OWN : (n + 1) * OWN]

                    @pl.when(jnp.logical_or(z != to, core != c))
                    def _():
                        src, dst = zs.at[n, pl.ds(0, OWN)], zr.at[core * NZ + z, pl.ds(0, OWN)]
                        remote(src, dst, z_send, z_recv, device(x, y, to, c)).start()

    def meet_line(p):
        if p == 0:

            @pl.when(core == 1)
            def _():
                pl.semaphore_wait(barrier, 2 * (NZ - 1))
                signal(line_in, device(x, y, z, 0))

        else:

            @pl.when(core == 0)
            def _():
                pl.semaphore_wait(line_in, 1)

    steps = {"c": swap_cores, "x": along_x, "y": along_y, "z": along_z, "m": meet_line}
    for step in ORDER:
        steps[step[0]](int(step[1:]))

    zr[core * NZ + z, :OWN] = zs[z * 2 + core, :OWN]
    for p in range(len(PIECES)):
        swaps[p].wait_send()
        wait(xr[p], x_send.at[p])
        wait(yr[p].at[pl.ds(0, GROUP - 1)], y_send.at[p])

        @pl.when(y // GROUP != PIECES[p][0])
        def _():
            wait(yr[p].at[0], y_send.at[p])

    all_but_one = zr.at[pl.ds(0, 2 * NZ - 1), pl.ds(0, OWN)]
    wait(all_but_one, z_send)
    wait(all_but_one, z_recv)
    for t in range(2):
        s = zr[t * NZ, :OWN]
        for d in range(1, NZ):
            s += zr[t * NZ + d, :OWN]
        out[t, :OWN] = s


def per_device(x_normed, key_grad, value_grad):
    hbm = pl.BlockSpec(memory_space=pl.ANY)
    vmem = pl.BlockSpec(memory_space=pltpu.VMEM)
    dma = pltpu.SemaphoreType.DMA
    count = len(PIECES)

    def buffers(*dims, dtype=bf16):
        return [pltpu.VMEM((*dims, height, HEAD), dtype) for height in HEIGHTS]

    both = pl.pallas_call(
        kernel,
        out_shape=jax.ShapeDtypeStruct((2, 8, HEAD), f32),
        in_specs=[hbm] * 3,
        out_specs=vmem,
        scratch_shapes=[
            pltpu.VMEM((TOK, D_WIN), bf16),
            pltpu.VMEM((2, TOK, HEAD), bf16),
            buffers(NX, GROUP),
            buffers(NX, GROUP),
            buffers(NX, GROUP),
            buffers(NX, GROUP),
            buffers(NX - 1, GROUP),
            buffers(GROUP, dtype=f32),
            buffers(GROUP),
            buffers(NY - 1),
            pltpu.VMEM((128, HEAD), f32),
            pltpu.VMEM((2 * NZ, 8, HEAD), f32),
            pltpu.VMEM((2 * NZ, 8, HEAD), f32),
            dma((2 + len(LOADS),)),
            dma((count,)),
            dma((count,)),
            dma((count,)),
            dma((count,)),
            dma((count,)),
            dma((count,)),
            dma,
            dma,
            pltpu.SemaphoreType.REGULAR,
            pltpu.SemaphoreType.REGULAR,
        ],
        compiler_params=pltpu.CompilerParams(
            collective_id=0, has_side_effects=True, vmem_limit_bytes=55140 * 1024
        ),
    )(x_normed, key_grad, value_grad)
    return both[0, :OWN], both[1, :OWN]


def solution(mesh):
    rows = P(("outer", "inner"), None)
    return jax.shard_map(per_device, mesh=mesh, in_specs=(rows,) * 3, out_specs=(rows, rows), check_vma=False)
```

time: 39.4 us -> 35.9 us (0.911)
  the two profiles are of different devices: /device:TPU:193 before, /device:TPU:1 now
where the time goes in v3:
time: 35.9 us; the launch traced here: 35.7 us
  Pallas kernels  34.5 us (96%)
  between operations  0.64 us (2%)
  local copies, waits for them, and re-layouts  0.6 us (2%)
    pallas_call x1, Pallas kernels, per_device(): pl.pallas_call(kernel, out_shape=jax.ShapeDtypeStruct((2, 8, HEAD), f32),...  34.5 us

profile of v3, /device:TPU:1, one launch (start us, length us, event | category | flops | bytes accessed | tf_op | source)
XLA Modules:
  0.0 35.7 jit_solution(6410937427070277842)
XLA Ops:
  0.6 34.5 %shard_map.50 = f32[2,8,128]{2,1,0:T(8,128)S(1)} custom-call(bf16[512,3840]{1,0:T(8,128)(2,1)} %x_hbm.1, bf16[512,128]{1,0:T(8,128)(2,1)} %k_hbm.1, bf16[512,128]{1,0:T(8,128)(2,1)} %v_hbm.1), custom_call_target="tpu_custom_call" | custom-call | tf_op jit(solution)/shard_map/pallas_call | solution.py:202
  35.1 0.6 %slice_bitcast_fusion = (f32[5,128]{1,0:T(8,128)}, f32[5,128]{1,0:T(8,128)}) fusion(f32[2,8,128]{2,1,0:T(8,128)S(1)} %shard_map.50), kind=kLoop, calls=%fused_computation | loop fusion | bytes 10240 | tf_op jit(solution)/shard_map/squeeze | solution.py:237

commit v4 on v3

--- a/solution.py
+++ b/solution.py
@@ -13,14 +13,21 @@
 LOADS = (2560, 1280)
 COLS = 256
 PIECES = (
-    (0, 0, 16), (0, 16, 32), (1, 0, 16), (0, 32, 48), (1, 16, 32), (0, 48, 64), (1, 32, 64), (0, 64, 96), (1, 64, 80), (0, 96, 120), (1, 80, 120),
+    ((0, 4), 0, 16),
+    ((4, 4), 0, 16),
+    ((0, 4), 16, 32),
+    ((0, 4), 32, 64),
+    ((4, 4), 16, 48),
+    ((0, 4), 64, 96),
+    ((4, 4), 48, 80),
+    ((0, 4), 96, 120),
+    ((4, 4), 80, 120),
 )
 HEIGHTS = tuple(-(-(hi - lo) // 16) * 16 for _, lo, hi in PIECES)
-GROUP = 4
 ORDER = (
-    "c0", "c1", "x0", "c2", "x1", "c3", "x2", "c4", "x3", "c5", "x4", "c6", "x5", "c7", "x6", "c8", "x7", "y0",
-    "c9", "x8", "c10", "x9", "y1", "x10", "y2", "y3", "m0", "y4", "y5", "m1", "z0", "y6", "z1", "z2", "y7",
-    "z3", "z4", "z5", "y8", "z6", "y9", "z7", "z8", "y10", "z9", "z10",
+    "x0", "c1", "c2", "x1", "c3", "x2", "c4", "x3", "c5", "x4", "c6", "x5", "c7", "x6", "c8", "x7", "y0", "x8",
+    "y1", "y2", "m0", "y3", "y4", "m1", "z0", "z1", "z2", "y5", "z3", "y6", "z4", "z5", "y7", "z6", "y8", "z7",
+    "z8",
 )
 bf16, f32 = jnp.bfloat16, jnp.float32
 
@@ -84,9 +91,9 @@
             for block in range(start // ROWS, -(-stop // ROWS)):
                 for p, (group, lo, hi) in enumerate(PIECES):
                     first, last = max(start, block * ROWS + lo), min(stop, block * ROWS + hi)
-                    if first < last and block % NY // GROUP == group:
+                    if first < last and 0 <= block % NY - group[0] < group[1]:
                         at = first - block * ROWS - lo
-                        dest[p][block // NY, block % GROUP, at : at + last - first, :] = half[first - start : last - start]
+                        dest[p][block // NY, block % NY - group[0], at : at + last - first, :] = half[first - start : last - start]
 
 
     @pl.when(core == 1)
@@ -102,13 +109,25 @@
         pltpu.make_async_copy(ref, ref, sem).wait()
 
     swaps = [
-        remote(give[p], got[p], core_send.at[p], core_recv.at[p], device(x, y, z, other)) for p in range(len(PIECES))
+        remote(give[p], got[p], core_send.at[p], core_recv.at[p], device(x, y, z, other)) if p else None
+        for p in range(len(PIECES))
     ]
 
     def swap_cores(p):
         swaps[p].start()
 
+    def in_group(p):
+        first, count = PIECES[p][0]
+        return jnp.logical_and(y >= first, y < first + count)
+
     def along_x(p):
+        if p == 0:
+            for d in (2, 1, 3):
+                to = (x + d) % NX
+                remote(keep[0].at[to], xr[0].at[d - 1], x_send.at[0], x_recv.at[0], device(to, y, z, core)).start()
+                remote(give[0].at[to], xr[0].at[d + 2], x_send.at[0], x_recv.at[0], device(to, y, z, other)).start()
+            remote(give[0].at[x], xr[0].at[6], x_send.at[0], x_recv.at[0], device(x, y, z, other)).start()
+            return
         swaps[p].wait_recv()
         for n in range(NX):
             xs[p][n] = (keep[p][n].astype(f32) + got[p][n].astype(f32)).astype(bf16)
@@ -118,13 +137,16 @@
 
     def along_y(p):
         wait(xr[p], x_recv.at[p])
-        s = keep[p][x].astype(f32) + got[p][x].astype(f32)
-        for d in range(NX - 1):
+        s = keep[p][x].astype(f32)
+        if p > 0:
+            s += got[p][x].astype(f32)
+        for d in range(xr[p].shape[0]):
             s += xr[p][d].astype(f32)
         yf[p][...] = s
         ys[p][...] = s.astype(bf16)
-        for n in range(GROUP):
-            to = PIECES[p][0] * GROUP + n
+        group = PIECES[p][0]
+        for n in range(group[1]):
+            to = group[0] + n
 
             @pl.when(y != to)
             def _():
@@ -132,10 +154,10 @@
                 remote(ys[p].at[n], yr[p].at[slot], y_send.at[p], y_recv.at[p], device(x, to, z, core)).start()
 
     def along_z(p):
-        @pl.when(y // GROUP == PIECES[p][0])
+        @pl.when(in_group(p))
         def _():
             wait(yr[p], y_recv.at[p])
-            s = yf[p][y % GROUP]
+            s = yf[p][y - PIECES[p][0][0]]
             for d in range(NY - 1):
                 s += yr[p][d].astype(f32)
             _, lo, hi = PIECES[p]
@@ -172,11 +194,12 @@
 
     zr[core * NZ + z, :OWN] = zs[z * 2 + core, :OWN]
     for p in range(len(PIECES)):
-        swaps[p].wait_send()
+        if p > 0:
+            swaps[p].wait_send()
         wait(xr[p], x_send.at[p])
-        wait(yr[p].at[pl.ds(0, GROUP - 1)], y_send.at[p])
-
-        @pl.when(y // GROUP != PIECES[p][0])
+        wait(yr[p].at[pl.ds(0, PIECES[p][0][1] - 1)], y_send.at[p])
+
+        @pl.when(jnp.logical_not(in_group(p)))
         def _():
             wait(yr[p].at[0], y_send.at[p])
 
@@ -196,8 +219,11 @@
     dma = pltpu.SemaphoreType.DMA
     count = len(PIECES)
 
-    def buffers(*dims, dtype=bf16):
-        return [pltpu.VMEM((*dims, height, HEAD), dtype) for height in HEIGHTS]
+    def buffers(*dims, dtype=bf16, owners=True):
+        return [
+            pltpu.VMEM((*dims, *((group[1],) if owners else ()), height, HEAD), dtype)
+            for (group, _, _), height in zip(PIECES, HEIGHTS)
+        ]
 
     both = pl.pallas_call(
         kernel,
@@ -207,14 +233,14 @@
         scratch_shapes=[
             pltpu.VMEM((TOK, D_WIN), bf16),
             pltpu.VMEM((2, TOK, HEAD), bf16),
-            buffers(NX, GROUP),
-            buffers(NX, GROUP),
-            buffers(NX, GROUP),
-            buffers(NX, GROUP),
-            buffers(NX - 1, GROUP),
-            buffers(GROUP, dtype=f32),
-            buffers(GROUP),
-            buffers(NY - 1),
+            buffers(NX),
+            buffers(NX),
+            buffers(NX),
+            buffers(NX),
+            buffers(2 * NX - 1)[:1] + buffers(NX - 1)[1:],
+            buffers(dtype=f32),
+            buffers(),
+            buffers(NY - 1, owners=False),
             pltpu.VMEM((128, HEAD), f32),
             pltpu.VMEM((2 * NZ, 8, HEAD), f32),
             pltpu.VMEM((2 * NZ, 8, HEAD), f32),

time: 35.9 us -> 35.2 us (0.981)
  Pallas kernels: 34.5 us -> 33.9 us
    pallas_call x1, Pallas kernels: 34.5 us -> 33.9 us  [per_device(): pl.pallas_call(kernel, out_shape=jax.ShapeDtypeStruct((2, 8, HEAD), f32),...]
where the time goes in v4:
time: 35.2 us; the launch traced here: 35.1 us
  Pallas kernels  33.9 us (96%)
  between operations  0.64 us (2%)
  local copies, waits for them, and re-layouts  0.6 us (2%)
    pallas_call x1, Pallas kernels, per_device(): pl.pallas_call(kernel, out_shape=jax.ShapeDtypeStruct((2, 8, HEAD), f32),...  33.9 us

profile of v4, /device:TPU:1, one launch (start us, length us, event | category | flops | bytes accessed | tf_op | source)
XLA Modules:
  0.0 35.1 jit_solution(13096580126300284495)
XLA Ops:
  0.6 33.9 %shard_map.50 = f32[2,8,128]{2,1,0:T(8,128)S(1)} custom-call(bf16[512,3840]{1,0:T(8,128)(2,1)} %x_hbm.1, bf16[512,128]{1,0:T(8,128)(2,1)} %k_hbm.1, bf16[512,128]{1,0:T(8,128)(2,1)} %v_hbm.1), custom_call_target="tpu_custom_call" | custom-call | tf_op jit(solution)/shard_map/pallas_call | solution.py:228
  34.5 0.6 %slice_bitcast_fusion = (f32[5,128]{1,0:T(8,128)}, f32[5,128]{1,0:T(8,128)}) fusion(f32[2,8,128]{2,1,0:T(8,128)S(1)} %shard_map.50), kind=kLoop, calls=%fused_computation | loop fusion | bytes 10240 | tf_op jit(solution)/shard_map/squeeze | solution.py:263

commit v5 on v4

--- a/solution.py
+++ b/solution.py
@@ -25,7 +25,7 @@
 )
 HEIGHTS = tuple(-(-(hi - lo) // 16) * 16 for _, lo, hi in PIECES)
 ORDER = (
-    "x0", "c1", "c2", "x1", "c3", "x2", "c4", "x3", "c5", "x4", "c6", "x5", "c7", "x6", "c8", "x7", "y0", "x8",
+    "x0", "c1", "c2", "c3", "c4", "c5", "c6", "c7", "c8", "x1", "x2", "x3", "x4", "x5", "x6", "x7", "y0", "x8",
     "y1", "y2", "m0", "y3", "y4", "m1", "z0", "z1", "z2", "y5", "z3", "y6", "z4", "z5", "y7", "z6", "y8", "z7",
     "z8",
 )

time: 35.2 us -> 35 us (level)
  no operation moved by 1% of the time
where the time goes in v5:
time: 35 us; the launch traced here: 34.9 us
  Pallas kernels  33.6 us (96%)
  between operations  0.64 us (2%)
  local copies, waits for them, and re-layouts  0.6 us (2%)
    pallas_call x1, Pallas kernels, per_device(): pl.pallas_call(kernel, out_shape=jax.ShapeDtypeStruct((2, 8, HEAD), f32),...  33.6 us

profile of v5, /device:TPU:1, one launch (start us, length us, event | category | flops | bytes accessed | tf_op | source)
XLA Modules:
  0.0 34.9 jit_solution(9034974956512673584)
XLA Ops:
  0.6 33.6 %shard_map.50 = f32[2,8,128]{2,1,0:T(8,128)S(1)} custom-call(bf16[512,3840]{1,0:T(8,128)(2,1)} %x_hbm.1, bf16[512,128]{1,0:T(8,128)(2,1)} %k_hbm.1, bf16[512,128]{1,0:T(8,128)(2,1)} %v_hbm.1), custom_call_target="tpu_custom_call" | custom-call | tf_op jit(solution)/shard_map/pallas_call | solution.py:228
  34.3 0.6 %slice_bitcast_fusion = (f32[5,128]{1,0:T(8,128)}, f32[5,128]{1,0:T(8,128)}) fusion(f32[2,8,128]{2,1,0:T(8,128)S(1)} %shard_map.50), kind=kLoop, calls=%fused_computation | loop fusion | bytes 10240 | tf_op jit(solution)/shard_map/squeeze | solution.py:263
